TPU v7x, 512 devices: a whole 4x4x16 slice. The times are simulated.
512 devices in a mesh: gy: 32 (over y, x, core), gz: 16 (over z).
Axes of the slice: x: 4, y: 4, z: 16, core: 2. Of those that a mesh axis runs over, the one named last changes fastest.
Arguments:
- strain: float32 [6, 192, 192, 512], P(None, 'gy', 'gz'), may hold values from -8 to 8
- phase: int32 [192, 192, 512], P('gy', 'gz'), may hold values from 0 to 15
- density: float32 [16], replicated, may hold values from 0.1 to 1
- target_stress: float32 [6], replicated, may hold values from -1.5 to 1.5
Outputs:
- next_strain: float32 [6, 192, 192, 512], P(None, 'gy', 'gz')
All inputs are finite; a program needn't handle non-finite values.
Results may differ from a plain program's by a relative error of at most 0.0001.
Values sent between devices are 32-bit elements; how exact they have to be, the bound alone decides.
A program may use at most 128 MiB of HBM per device.

v0:
```python
import math

import jax
import jax.numpy as jnp
from jax import lax
from jax.sharding import PartitionSpec as P

NX = 512
NY = 192
NZ = 192


LAME_SOLID = 0.5769230769
SHEAR_SOLID = 0.3846153846
PAIRS = ((0, 0), (1, 1), (2, 2), (1, 2), (0, 2), (0, 1))
INDEX_MAP = ((0, 5, 4), (5, 1, 3), (4, 3, 2))
HIGHEST = lax.Precision.HIGHEST


def signed_wave(wave_ids, length):
    return jnp.where(wave_ids > length // 2, wave_ids - length, wave_ids)


def wave_table(wave_ids, length):
    grid = jnp.arange(length, dtype=jnp.int32)
    turns = wave_ids[:, None] * grid[None, :] % length
    angle = turns.astype(jnp.float32) * (2.0 * math.pi / length)
    return (jnp.cos(angle), jnp.sin(angle))


def forward_table(length):
    cosine, sine = wave_table(jnp.arange(length, dtype=jnp.int32), length)
    real_row = jnp.stack([cosine, sine], axis=1)
    imag_row = jnp.stack([-sine, cosine], axis=1)
    return jnp.stack([real_row, imag_row])


def inverse_table(length):
    cosine, sine = wave_table(jnp.arange(length, dtype=jnp.int32), length)
    real_row = jnp.stack([cosine, -sine])
    imag_row = jnp.stack([sine, cosine])
    return jnp.stack([real_row, imag_row])


def contract(form, left, right):
    return jnp.einsum(form, left, right, precision=HIGHEST, preferred_element_type=jnp.float32)


def green_part(spectrum, frequency, keep_mask, safe_norm, shear_ref, coupling):
    vector = [sum((spectrum[INDEX_MAP[i][j]] * frequency[j] for j in range(3))) for i in range(3)]
    projected = frequency[0] * vector[0] + frequency[1] * vector[1] + frequency[2] * vector[2]
    scaled = [
        jnp.where(keep_mask, vector[i] / (2.0 * shear_ref * safe_norm), 0.0) for i in range(3)
    ]
    fourth = jnp.where(keep_mask, coupling * projected / (safe_norm * safe_norm), 0.0)
    images = [
        frequency[i] * scaled[j] + frequency[j] * scaled[i] - frequency[i] * frequency[j] * fourth
        for i, j in PAIRS
    ]
    return jnp.stack(images)


def local(strain, phase, density, target_stress):
    components, local_y, local_z, length_x = strain.shape
    n_gy = lax.axis_size("gy")
    n_gz = lax.axis_size("gz")
    voxels = float(NX * NY * NZ)
    stiff_scale = density**3
    level_ids = jnp.arange(density.shape[0], dtype=jnp.int32)
    level_hit = phase[None] == level_ids[:, None, None, None]
    stiffness = jnp.sum(jnp.where(level_hit, stiff_scale[:, None, None, None], 0.0), axis=0)
    lame_cell = LAME_SOLID * stiffness
    shear_cell = SHEAR_SOLID * stiffness
    middle = 0.5 * (jnp.min(stiff_scale) + jnp.max(stiff_scale))
    lame_ref = LAME_SOLID * middle
    shear_ref = SHEAR_SOLID * middle
    strain_trace = strain[0] + strain[1] + strain[2]
    diagonal = (jnp.arange(6) < 3).astype(jnp.float32)
    diagonal_grid = diagonal[:, None, None, None]
    stress = diagonal_grid * (lame_cell * strain_trace)[None] + 2.0 * shear_cell[None] * strain
    polarize = (
        diagonal_grid * ((lame_cell - lame_ref) * strain_trace)[None]
        + 2.0 * (shear_cell - shear_ref)[None] * strain
    )
    strain_total, stress_total = lax.psum(
        (jnp.sum(strain, axis=(1, 2, 3)), jnp.sum(stress, axis=(1, 2, 3))), ("gy", "gz")
    )
    excess = target_stress - stress_total / voxels
    excess_trace = excess[0] + excess[1] + excess[2]
    macro_strain = strain_total / voxels + (
        excess - diagonal * lame_ref / (3.0 * lame_ref + 2.0 * shear_ref) * excess_trace
    ) / (2.0 * shear_ref)
    x_weight = jnp.ones((length_x,), jnp.float32)
    x_inner = length_x // n_gy
    y_inner = NY // n_gz
    columns = y_inner * x_inner
    local_rows = components * local_y * local_z
    x_cos, x_sin = wave_table(jnp.arange(length_x, dtype=jnp.int32), length_x)
    x_forward = jnp.concatenate([x_cos, -x_sin], axis=0)
    flat_field = polarize.reshape(local_rows, length_x)
    x_spectrum = contract("kn,mn->km", x_forward, flat_field).reshape(2, n_gy, x_inner, local_rows)
    y_lines = lax.all_to_all(x_spectrum, "gy", split_axis=1, concat_axis=1, tiled=True)
    y_lines = y_lines.reshape(2, n_gy, x_inner, components, local_y, local_z)
    y_lines = jnp.transpose(y_lines, (0, 2, 3, 5, 1, 4)).reshape(
        2, x_inner * components * local_z, NY
    )
    y_spectrum = contract("rkpy,pmy->rkm", forward_table(NY), y_lines)
    y_spectrum = y_spectrum.reshape(2, n_gz, y_inner, x_inner * components * local_z)
    z_lines = lax.all_to_all(y_spectrum, "gz", split_axis=1, concat_axis=1, tiled=True)
    z_lines = z_lines.reshape(2, n_gz, y_inner, x_inner, components, local_z)
    z_lines = jnp.transpose(z_lines, (0, 4, 2, 3, 1, 5)).reshape(2, components, columns, NZ)
    z_spectrum = contract("rkpz,pcmz->rckm", forward_table(NZ), z_lines)
    wave_z = jnp.arange(NZ, dtype=jnp.int32)
    column_ids = jnp.arange(columns, dtype=jnp.int32)
    wave_y = lax.axis_index("gz") * y_inner + column_ids // x_inner
    wave_x = lax.axis_index("gy") * x_inner + column_ids % x_inner
    freq_z = (signed_wave(wave_z, NZ).astype(jnp.float32) / NZ)[:, None]
    freq_y = (signed_wave(wave_y, NY).astype(jnp.float32) / NY)[None, :]
    freq_x = (signed_wave(wave_x, NX).astype(jnp.float32) / NX)[None, :]
    plane = (NZ, columns)
    frequency = (
        jnp.broadcast_to(freq_x, plane),
        jnp.broadcast_to(freq_y, plane),
        jnp.broadcast_to(freq_z, plane),
    )
    keep_mask = (
        (wave_z != NZ // 2)[:, None] & (wave_y != NY // 2)[None, :] & (wave_x != NX // 2)[None, :]
    )
    keep_mask = keep_mask & jnp.logical_not(
        (wave_z == 0)[:, None] & (wave_y == 0)[None, :] & (wave_x == 0)[None, :]
    )
    norm_sq = frequency[0] ** 2 + frequency[1] ** 2 + frequency[2] ** 2
    safe_norm = jnp.where(keep_mask, norm_sq, 1.0)
    coupling = (lame_ref + shear_ref) / (shear_ref * (lame_ref + 2.0 * shear_ref))
    g_real = green_part(z_spectrum[0], frequency, keep_mask, safe_norm, shear_ref, coupling)
    g_imag = green_part(z_spectrum[1], frequency, keep_mask, safe_norm, shear_ref, coupling)
    green = jnp.stack([g_real, g_imag])
    z_back = contract("rpkz,pckm->rzcm", inverse_table(NZ), green)
    z_back = z_back.reshape(2, n_gz, local_z, components * columns)
    back_z = lax.all_to_all(z_back, "gz", split_axis=1, concat_axis=1, tiled=True)
    back_z = back_z.reshape(2, n_gz, local_z, components, y_inner, x_inner)
    back_z = jnp.transpose(back_z, (0, 5, 3, 2, 1, 4)).reshape(
        2, x_inner * components * local_z, NY
    )
    y_back = contract("rpky,pmk->rym", inverse_table(NY), back_z)
    y_back = y_back.reshape(2, n_gy, local_y, x_inner * components * local_z)
    back_y = lax.all_to_all(y_back, "gy", split_axis=1, concat_axis=1, tiled=True)
    back_y = back_y.reshape(2, n_gy, local_y, x_inner, components, local_z)
    back_y = jnp.transpose(back_y, (4, 2, 5, 0, 1, 3)).reshape(local_rows, 2 * length_x)
    x_scale = (x_weight / voxels)[:, None]
    x_inverse = jnp.concatenate([x_cos * x_scale, -x_sin * x_scale], axis=0)
    fluctuation = contract("mk,kn->mn", back_y, x_inverse).reshape(
        components, local_y, local_z, length_x
    )
    return macro_strain[:, None, None, None] - fluctuation


def solution(mesh):
    placed = (P(None, "gy", "gz", None), P("gy", "gz", None), P(), P())
    return jax.shard_map(
        local, mesh=mesh, in_specs=placed, out_specs=P(None, "gy", "gz", None), check_vma=False
    )
```

profile of v0, /device:TPU:1, one launch (start us, length us, event | category | flops | bytes accessed | tf_op | source)
XLA Modules:
  0.0 576.2 jit_solution(16038826592424755981)
XLA Ops:
  0.0 4.1 sine_negate_fusion
  4.2 0.6 fusion.119
  6.0 0.7 select_reduce_fusion
  7.2 1.2 fusion.121
  8.4 1.0 reshape.6659
  9.6 1.0 copy-done
  10.6 4.8 fusion.9
  15.4 10.9 %all-to-all-start = ((f32[2,32,16,432]{3,2,0,1:T(8,128)}), f32[2,32,16,432]{3,2,0,1:T(8,128)S(1)}, u32[]{:S(2)}, u32[]{:S(2)}) async-start(f32[2,32,16,432]{3,2,0,1:T(8,128)} %fusion.9), calls=%async_computation | async-start | bytes 4194304 | tf_op jit(solution)/shard_map/all_to_all | solution.py:102
  26.3 0.9 fusion.83
  27.1 26.9 %all-to-all-done = f32[2,32,16,432]{3,2,0,1:T(8,128)S(1)} async-done(((f32[2,32,16,432]{3,2,0,1:T(8,128)}), f32[2,32,16,432]{3,2,0,1:T(8,128)S(1)}, u32[]{:S(2)}, u32[]{:S(2)}) %all-to-all-start) | async-done | bytes 1769504 | tf_op jit(solution)/shard_map/all_to_all | solution.py:102
  54.1 4.4 copy.103
  58.5 21.7 %copy.104 = f32[2,16,6,12,32,6]{3,2,1,5,4,0:T(8,128)} copy(f32[2,16,6,12,32,6]{4,1,3,5,2,0:T(8,128)} %bitcast.313) | data formatting | bytes 3538944 | tf_op jit(solution)/shard_map/transpose | solution.py:104
  80.2 15.0 %reshape.6660 = f32[2,1152,192,1,1]{1,2,0,3,4:T(8,128)S(1)} reshape(f32[2,16,6,12,32,6]{3,2,1,5,4,0:T(8,128)} %copy.104) | data formatting | bytes 3538944 | tf_op jit(solution)/shard_map/reshape | solution.py:104
  95.2 3.2 convolution_bitcast_fusion.1
  98.4 2.6 copy.105
  101.0 13.3 %all-to-all-start.1 = ((f32[2,16,12,1152]{3,0,2,1:T(2,128)}), f32[2,16,12,1152]{3,0,2,1:T(2,128)S(1)}, u32[]{:S(2)}, u32[]{:S(2)}) async-start(f32[2,16,12,1152]{3,0,2,1:T(2,128)} %copy.105), calls=%async_computation.1 | async-start | bytes 3538944 | tf_op jit(solution)/shard_map/all_to_all | solution.py:109
  114.4 0.6 iota_compare_fusion.1
  116.6 0.6 fusion.98
  119.0 0.6 fusion.112
  119.6 0.8 fusion.93
  120.3 0.8 fusion.92
  121.1 0.8 fusion.79
  121.9 0.8 fusion.87
  122.7 0.9 maximum_bitcast_fusion.12
  123.7 0.9 maximum_bitcast_fusion.10
  124.6 67.5 %all-to-all-done.1 = f32[2,16,12,1152]{3,0,2,1:T(2,128)S(1)} async-done(((f32[2,16,12,1152]{3,0,2,1:T(2,128)}), f32[2,16,12,1152]{3,0,2,1:T(2,128)S(1)}, u32[]{:S(2)}, u32[]{:S(2)}) %all-to-all-start.1) | async-done | bytes 1769504 | tf_op jit(solution)/shard_map/all_to_all | solution.py:109
  192.4 14.7 %reshape.6653 = f32[2,16,12,16,6,12]{5,4,3,1,2,0:T(8,128)} reshape(f32[2,16,12,1152]{3,1,2,0:T(8,128)S(1)} %copy.106) | data formatting | bytes 3538944 | tf_op jit(solution)/shard_map/reshape | solution.py:110
  207.1 20.6 %copy.141 = f32[2,6,12,16,16,12]{5,4,3,2,0,1:T(8,128)} copy(f32[2,6,12,16,16,12]{5,1,3,4,2,0:T(8,128)} %bitcast.311) | data formatting | bytes 3538944 | tf_op jit(solution)/shard_map/reshape | solution.py:111
  227.8 13.7 %reshape.6662 = f32[2,6,192,192,1]{3,2,0,1,4:T(8,128)S(1)} reshape(f32[2,6,12,16,16,12]{5,4,3,2,0,1:T(8,128)} %copy.141) | data formatting | bytes 3538944 | tf_op jit(solution)/shard_map/reshape | solution.py:111
  241.5 4.0 fusion.13
  248.8 4.0 fusion.12
  252.8 1.4 copy.121
  254.3 2.9 reshape.6655
  257.1 11.5 %all-to-all-start.2 = ((f32[2,16,12,1152]{3,0,2,1:T(2,128)}), f32[2,16,12,1152]{3,0,2,1:T(2,128)S(1)}, u32[]{:S(2)}, u32[]{:S(2)}) async-start(f32[2,16,12,1152]{3,0,2,1:T(2,128)} %reshape.6655), calls=%async_computation.2 | async-start | bytes 3538944 | tf_op jit(solution)/shard_map/all_to_all | solution.py:140
  268.7 1.5 copy.101
  270.2 75.6 %all-to-all-done.2 = f32[2,16,12,1152]{3,0,2,1:T(2,128)S(1)} async-done(((f32[2,16,12,1152]{3,0,2,1:T(2,128)}), f32[2,16,12,1152]{3,0,2,1:T(2,128)S(1)}, u32[]{:S(2)}, u32[]{:S(2)}) %all-to-all-start.2) | async-done | bytes 1769504 | tf_op jit(solution)/shard_map/all_to_all | solution.py:140
  346.1 11.0 %reshape.6656 = f32[2,16,12,6,12,16]{5,4,3,1,2,0:T(8,128)} reshape(f32[2,16,12,1152]{3,1,2,0:T(8,128)S(1)} %copy.122) | data formatting | bytes 3538944 | tf_op jit(solution)/shard_map/reshape | solution.py:141
  357.2 23.5 %copy.123 = f32[2,16,6,12,16,12]{5,4,3,2,1,0:T(8,128)} copy(f32[2,16,6,12,16,12]{1,5,2,4,3,0:T(8,128)} %bitcast.312) | data formatting | bytes 3538944 | tf_op jit(solution)/shard_map/transpose | solution.py:142
  380.7 13.5 %reshape.6657 = f32[2,1152,192]{2,1,0:T(8,128)S(1)} reshape(f32[2,16,6,12,16,12]{5,4,3,2,1,0:T(8,128)} %copy.123) | data formatting | bytes 3538944 | tf_op jit(solution)/shard_map/reshape | solution.py:142
  394.2 3.4 convolution_bitcast_fusion
  397.6 2.6 copy.126
  400.2 11.6 %all-to-all-start.3 = ((f32[2,32,6,1152]{3,0,2,1:T(2,128)}), f32[2,32,6,1152]{3,0,2,1:T(2,128)S(1)}, u32[]{:S(2)}, u32[]{:S(2)}) async-start(f32[2,32,6,1152]{3,0,2,1:T(2,128)} %copy.126), calls=%async_computation.3 | async-start | bytes 3538944 | tf_op jit(solution)/shard_map/all_to_all | solution.py:147
  411.8 115.1 %all-reduce = (f32[6]{0:T(128)S(1)}, f32[6]{0:T(128)S(1)}) all-reduce(f32[6]{0:T(128)S(1)} %copy-done.25, f32[6]{0:T(128)S(1)} %copy-done.24), channel_id=1, replica_groups=mesh['gy'=32,'gz'=16] {'gy','gz'}, use_global_device_ids=true, to_apply=%region_4.5 | all-reduce | flops 12 | bytes 96 | tf_op jit(solution)/shard_map/psum | solution.py:85
  529.4 5.4 broadcast_multiply_fusion
  534.7 8.3 %copy.127 = f32[2,32,6,1152]{1,0,3,2:T(2,128)} copy(f32[2,32,6,1152]{3,0,2,1:T(2,128)S(1)} %all-to-all-done.3) | data formatting | bytes 3538944 | tf_op jit(solution)/shard_map/all_to_all | solution.py:147
  543.0 14.9 %copy.128 = f32[6,6,12,2,32,16]{5,4,3,2,1,0:T(8,128)} copy(f32[6,6,12,2,32,16]{4,3,2,0,5,1:T(2,128)} %bitcast.314) | data formatting | bytes 3538944 | tf_op jit(solution)/shard_map/transpose | solution.py:149
  557.9 11.7 %dot_general.34 = f32[6,6,12,1024]{3,2,1,0:T(8,128)S(1)} reshape(f32[6,6,12,2,32,16]{5,4,3,2,1,0:T(8,128)} %copy.128) | data formatting | bytes 3538944 | tf_op jit(solution)/shard_map/mk,kn->mn/dot_general | solution.py:46
  569.7 6.1 %fusion.16 = f32[6,6,12,512]{3,2,1,0:T(8,128)} fusion(f32[6,6,12,1024]{3,2,1,0:T(8,128)S(1)} %dot_general.34, f32[512,512]{1,0:T(8,128)S(1)} %get-tuple-element.69, f32[512,512]{1,0:T(8,128)} %get-tuple-element.70, f32[6]{0:T(128)S(1)} %divide_add_fusion), kind=kOutput, calls=%fused_computation.24 | convolution fusion | flops 2718654464 | bytes 4751384 | tf_op jit(solution)/shard_map/mk,kn->mn/dot_general | solution.py:46
  (82 shorter events, 8.6 us)
Async XLA Ops:
  0.0 4.1 copy-start.26
  0.0 6.0 %copy-start.10 = (s32[6,12,512]{2,1,0:T(8,128)S(1)}, s32[6,12,512]{2,1,0:T(8,128)}, u32[]{:S(2)}) copy-start(s32[6,12,512]{2,1,0:T(8,128)} %param.5) | copy-start | bytes 442372
  0.0 6.8 %copy-start.6 = (f32[6,6,12,512]{3,2,1,0:T(8,128)S(1)}, f32[6,6,12,512]{3,2,1,0:T(8,128)}, u32[]{:S(2)}) copy-start(f32[6,6,12,512]{3,2,1,0:T(8,128)} %param.4) | copy-start | bytes 2654212
  6.0 1.3 copy-start.7
  9.4 1.2 copy-start
  15.4 38.7 %all-to-all-start = ((f32[2,32,16,432]{3,2,0,1:T(8,128)}), f32[2,32,16,432]{3,2,0,1:T(8,128)S(1)}, u32[]{:S(2)}, u32[]{:S(2)}) async-start(f32[2,32,16,432]{3,2,0,1:T(8,128)} %fusion.9), calls=%async_computation | async-start | bytes 4194304 | tf_op jit(solution)/shard_map/all_to_all | solution.py:102
  101.0 91.1 %all-to-all-start.1 = ((f32[2,16,12,1152]{3,0,2,1:T(2,128)}), f32[2,16,12,1152]{3,0,2,1:T(2,128)S(1)}, u32[]{:S(2)}, u32[]{:S(2)}) async-start(f32[2,16,12,1152]{3,0,2,1:T(2,128)} %copy.105), calls=%async_computation.1 | async-start | bytes 3538944 | tf_op jit(solution)/shard_map/all_to_all | solution.py:109
  227.7 13.7 %copy-start.8 = (f32[1,192,2,192]{3,1,2,0:T(8,128)S(1)}, f32[1,192,2,192]{3,1,2,0:T(8,128)}, u32[]{:S(2)}) copy-start(f32[1,192,2,192]{3,1,2,0:T(8,128)} %get-tuple-element.32) | copy-start | bytes 884740
  227.7 13.7 %copy-start.9 = (f32[1,192,2,192]{3,1,2,0:T(8,128)S(1)}, f32[1,192,2,192]{3,1,2,0:T(8,128)}, u32[]{:S(2)}) copy-start(f32[1,192,2,192]{3,1,2,0:T(8,128)} %get-tuple-element.33) | copy-start | bytes 884740
  241.5 4.1 copy-start.11
  241.5 4.1 copy-start.12
  241.5 4.1 copy-start.13
  241.5 4.1 copy-start.14
  241.5 4.1 copy-start.15
  241.5 4.1 copy-start.16
  241.5 4.1 copy-start.17
  241.5 4.1 copy-start.18
  241.5 4.1 copy-start.19
  245.6 0.8 copy-start.20
  245.6 0.8 copy-start.21
  246.0 0.7 copy-start.22
  247.6 0.7 copy-start.23
  247.7 1.0 copy-start.1
  247.7 1.1 copy-start.3
  257.1 11.5 %copy-start.2 = (f32[1,2,192,192]{2,3,1,0:T(8,128)S(1)}, f32[1,2,192,192]{2,3,1,0:T(8,128)}, u32[]{:S(2)}) copy-start(f32[1,2,192,192]{2,3,1,0:T(8,128)} %get-tuple-element.30) | copy-start | bytes 884740
  257.1 11.6 %copy-start.4 = (f32[1,2,192,192]{2,3,1,0:T(8,128)S(1)}, f32[1,2,192,192]{2,3,1,0:T(8,128)}, u32[]{:S(2)}) copy-start(f32[1,2,192,192]{2,3,1,0:T(8,128)} %get-tuple-element.31) | copy-start | bytes 884740
  257.1 88.7 %all-to-all-start.2 = ((f32[2,16,12,1152]{3,0,2,1:T(2,128)}), f32[2,16,12,1152]{3,0,2,1:T(2,128)S(1)}, u32[]{:S(2)}, u32[]{:S(2)}) async-start(f32[2,16,12,1152]{3,0,2,1:T(2,128)} %reshape.6655), calls=%async_computation.2 | async-start | bytes 3538944 | tf_op jit(solution)/shard_map/all_to_all | solution.py:140
  380.7 13.5 %copy-start.5 = (f32[2,192,192,2]{2,3,1,0:T(2,128)S(1)}, f32[2,192,192,2]{2,3,1,0:T(2,128)}, u32[]{:S(2)}) copy-start(f32[2,192,192,2]{2,3,1,0:T(2,128)} %copy.101) | copy-start | bytes 1769476
  400.2 11.6 %copy-start.24 = (f32[6]{0:T(128)S(1)}, f32[6]{0:T(128)}, u32[]{:S(2)}) copy-start(f32[6]{0:T(128)} %get-tuple-element.5) | copy-start | bytes 76
  400.2 11.6 %copy-start.25 = (f32[6]{0:T(128)S(1)}, f32[6]{0:T(128)}, u32[]{:S(2)}) copy-start(f32[6]{0:T(128)} %get-tuple-element.6) | copy-start | bytes 76
  400.2 126.7 %copy-start.27 = (f32[6]{0:T(128)S(1)}, f32[6]{0:T(128)}, u32[]{:S(2)}) copy-start(f32[6]{0:T(128)} %param.7) | copy-start | bytes 76
  400.2 134.5 %all-to-all-start.3 = ((f32[2,32,6,1152]{3,0,2,1:T(2,128)}), f32[2,32,6,1152]{3,0,2,1:T(2,128)S(1)}, u32[]{:S(2)}, u32[]{:S(2)}) async-start(f32[2,32,6,1152]{3,0,2,1:T(2,128)} %copy.126), calls=%async_computation.3 | async-start | bytes 3538944 | tf_op jit(solution)/shard_map/all_to_all | solution.py:147
where the time goes:
time: 586 us; the launch traced here: 576 us
  local copies, waits for them, and re-layouts  189 us (32%)
  waiting for transfers between devices  170 us (29%)
  blocking collectives  115 us (20%)
  starting transfers between devices  47.3 us (8%)
  other arithmetic  25.7 us (4%)
  matrix products  25.5 us (4%)
    psum x1, blocking collectives, local(): lax.psum((jnp.sum(strain, axis=(1, 2, 3)), jnp.sum(stress, axis=(1, 2, 3)...  115 us
    all_to_all x1, waiting for transfers between devices, local(): lax.all_to_all(z_back, 'gz', split_axis=1, concat_axis=1, tiled=True)  75.6 us
    all_to_all x1, waiting for transfers between devices, local(): lax.all_to_all(y_spectrum, 'gz', split_axis=1, concat_axis=1, tiled=True)  67.5 us
    reshape x2, local copies, waits for them, and re-layouts, local(): jnp.transpose(z_lines, (0, 4, 2, 3, 1, 5))  34.3 us
    all_to_all x1, waiting for transfers between devices, local(): lax.all_to_all(x_spectrum, 'gy', split_axis=1, concat_axis=1, tiled=True)  26.9 us
    dot_general x6, matrix products, contract(): jnp.einsum(form, left, right, precision=HIGHEST, preferred_element_type=j...  25.5 us
    transpose x1, local copies, waits for them, and re-layouts, local(): jnp.transpose(back_z, (0, 5, 3, 2, 1, 4))  23.5 us
    transpose x1, local copies, waits for them, and re-layouts, local(): jnp.transpose(y_lines, (0, 2, 3, 5, 1, 4))  21.7 us
  transfers between devices with their start and end apart: 4, of which 3 were waited for; matrix products, arithmetic and copies ran while one was open for 3% of the time, Pallas kernels for 0%

commit v1 on v0

v1 whole, which is shorter than its diff:
```python
import math

import jax
import jax.numpy as jnp
import ml_dtypes
import numpy as np
from jax import lax
from jax.experimental import pallas as pl
from jax.experimental.pallas import tpu as pltpu
from jax.sharding import PartitionSpec as P

NX, NY, NZ = 512, 192, 192
GY, GZ = 32, 16
YL, ZL = NY // GY, NZ // GZ
VOXELS = float(NX * NY * NZ)
LAME_SOLID = 0.5769230769
SHEAR_SOLID = 0.3846153846
MESH = pl.DeviceIdType.MESH
F32, BF16 = jnp.float32, jnp.bfloat16
TILES = 9
FORWARD = ((0, 5), (5, 9))
BACKWARD = ((0, 4), (4, 9))


def split_table(table, axis):
    high = table.astype(np.float32).astype(ml_dtypes.bfloat16)
    low = (table - high.astype(np.float64)).astype(np.float32).astype(ml_dtypes.bfloat16)
    return np.concatenate([high, high, low], axis=axis)


def wave(rows, columns, length):
    angle = 2.0 * math.pi / length * ((np.asarray(rows)[:, None] * np.asarray(columns)[None, :]) % length)
    return np.cos(angle), np.sin(angle)


def tables():
    kx = np.array([d * 16 + h * 8 + k for h in range(2) for d in range(GZ) for _ in range(2) for k in range(8)])
    imag = np.array([r for _ in range(2) for _ in range(GZ) for r in range(2) for _ in range(8)])
    cosine, sine = wave(np.arange(NX), kx, NX)
    x_table = np.where(imag[None, :] == 0, cosine, -sine)
    x_forward = split_table(x_table, 0)
    x_back = np.stack([split_table(x_table.T[h * 256 : (h + 1) * 256], 0) for h in range(2)])

    z_rows = np.arange(GZ * 16)
    z_of, z_ok = (z_rows // 16) * ZL + np.minimum(z_rows % 16, ZL - 1), z_rows % 16 < ZL
    k_rows = np.arange(GY * 8)
    k_of, k_ok = (k_rows // 8) * 6 + np.minimum(k_rows % 8, 5), k_rows % 8 < 6
    cosine, sine = wave(k_of, z_of, NZ)
    ok = k_ok[:, None] & z_ok[None, :]
    cosine, sine = np.where(ok, cosine, 0.0), np.where(ok, sine, 0.0)
    z_forward = split_table(np.concatenate([cosine, sine], axis=1), 1)
    z_back = split_table(np.concatenate([cosine.T, -sine.T], axis=1), 1)

    y_of = np.array([s * YL + y for y in range(YL) for s in range(GY)])
    cosine, sine = wave(np.arange(NY), y_of, NY)
    y_forward = split_table(np.concatenate([cosine, sine], axis=1), 1)
    y_back = split_table(np.concatenate([cosine.T, -sine.T], axis=1), 1)
    return x_forward, z_forward, y_forward, y_back, z_back, x_back


def lane_ids(rows):
    return lax.broadcasted_iota(jnp.int32, (rows, 128), 1)


def block_swap(arrays):
    rows = next(a for a in arrays if a is not None).shape[0]
    lane = lane_ids(rows)
    arrays = [jnp.zeros((rows, 128), F32) if a is None else a for a in arrays]
    for step in (4, 2, 1):
        width = 16 * step
        low = (lane // width) % 2 == 0
        out = list(arrays)
        for i in range(8):
            if (i // step) % 2 == 0:
                a, b = arrays[i], arrays[i + step]
                out[i] = jnp.where(low, a, pltpu.roll(b, width, 1))
                out[i + step] = jnp.where(low, pltpu.roll(a, 128 - width, 1), b)
        arrays = out
    return arrays


def turned(x):
    real = (lane_ids(x.shape[0]) // 8) % 2 == 0
    return jnp.where(real, pltpu.roll(x, 120, 1), -pltpu.roll(x, 8, 1))


def halves(x):
    high = x.astype(BF16)
    return high, (x - high.astype(F32)).astype(BF16)


def put_operand(ref, row, count, lanes, x):
    high, low = halves(x)
    turn_high, turn_low = halves(turned(x))
    size = x.shape[0]
    for block, value in enumerate((high, turn_high, low, turn_low, high, turn_high)):
        ref[pl.ds(row + block * count, size), lanes] = value


def dot(a, b):
    return jnp.dot(a, b, preferred_element_type=F32)


def kernel(
    strain, phase, density, target, x_table, z_fwd_hbm, y_fwd_hbm, y_back_hbm, z_back_hbm, x_back_hbm,
    out,
    z_fwd, y_fwd, y_back, z_back, x_back,
    field, x_left, x_spec,
    f_send, f_recv, g_send, g_recv, h_send, h_recv, b_send, b_recv,
    z_right, y_right, y_spec, y_lines, back_left,
    table_sem, f_ssem, f_rsem, g_ssem, g_rsem, h_ssem, h_rsem, b_ssem, b_rsem,
):
    gy, gz = lax.axis_index("gy"), lax.axis_index("gz")

    loads = [
        pltpu.make_async_copy(src, dst, table_sem.at[i])
        for i, (src, dst) in enumerate(
            ((z_fwd_hbm, z_fwd), (y_fwd_hbm, y_fwd), (y_back_hbm, y_back), (z_back_hbm, z_back), (x_back_hbm, x_back))
        )
    ]
    for load in loads:
        load.start()

    f_recv[...] = jnp.zeros_like(f_recv)
    h_recv[...] = jnp.zeros_like(h_recv)

    barrier = pltpu.get_barrier_semaphore()

    def greet(axis, me, n):
        def body(i, carry):
            pl.semaphore_signal(barrier, inc=1, device_id={axis: lax.rem(me + i, n)}, device_id_type=MESH)
            return carry

        lax.fori_loop(1, n, body, 0)

    greet("gz", gz, GZ)
    greet("gy", gy, GY)

    def transfer(axis, me, n, pad, used, src, dst, ssem, rsem, chunk, tiles):
        lo, hi = tiles

        def copy(i):
            hop = lax.div(i + 1, 2)
            there = lax.rem(me + jnp.where(lax.rem(i, 2) == 1, hop, n - hop), n)
            return pltpu.make_async_remote_copy(
                src_ref=src.at[lo:hi, pl.ds(pl.multiple_of(there * pad, pad), used), :],
                dst_ref=dst.at[lo:hi, pl.ds(pl.multiple_of(me * pad, pad), used), :],
                send_sem=ssem.at[chunk, i],
                recv_sem=rsem.at[chunk, i],
                device_id={axis: there},
                device_id_type=MESH,
            )

        def start():
            lax.fori_loop(1, n, lambda i, c: (copy(i).start(), c)[1], 0)
            own = pl.ds(pl.multiple_of(me * pad, pad), used)
            dst[lo:hi, own, :] = src[lo:hi, own, :]

        def wait_recv():
            lax.fori_loop(1, n, lambda i, c: (copy(i).wait_recv(), c)[1], 0)

        def wait_send():
            lax.fori_loop(1, n, lambda i, c: (copy(i).wait_send(), c)[1], 0)

        return start, wait_recv, wait_send

    to_z = [transfer("gz", gz, GZ, 16, ZL, f_send, f_recv, f_ssem, f_rsem, h, FORWARD[h]) for h in range(2)]
    to_y = [transfer("gy", gy, GY, 8, 6, g_send, g_recv, g_ssem, g_rsem, h, FORWARD[h]) for h in range(2)]
    from_y = [transfer("gy", gy, GY, 8, 6, h_send, h_recv, h_ssem, h_rsem, h, BACKWARD[h]) for h in range(2)]
    from_z = [transfer("gz", gz, GZ, 16, ZL, b_send, b_recv, b_ssem, b_rsem, h, BACKWARD[h]) for h in range(2)]

    cubes = [density[i] * density[i] * density[i] for i in range(16)]
    least, most = cubes[0], cubes[0]
    for value in cubes[1:]:
        least, most = jnp.minimum(least, value), jnp.maximum(most, value)
    middle = 0.5 * (least + most)
    lame_ref, shear_ref = LAME_SOLID * middle, SHEAR_SOLID * middle

    field[...] = jnp.zeros_like(field)

    def polarize(y, carry):
        level = phase[y]
        stiff = jnp.zeros(level.shape, F32)
        for i, value in enumerate(cubes):
            stiff = jnp.where(level == i, value, stiff)
        excess = stiff - middle
        parts = [strain[c, y] for c in range(6)]
        trace = LAME_SOLID * (parts[0] + parts[1] + parts[2])
        for c in range(6):
            value = (2.0 * SHEAR_SOLID) * parts[c]
            field[c * YL + y, 0:ZL, :] = excess * (value + trace if c < 3 else value)
        return carry

    lax.fori_loop(0, YL, polarize, 0)

    def split_rows(g, carry):
        high, low = halves(field[g])
        rows = pl.ds(pl.multiple_of(g * 16, 16), 16)
        x_left[rows, 0:512] = high
        x_left[rows, 512:1024] = low
        x_left[rows, 1024:1536] = high
        return carry

    lax.fori_loop(0, 36, split_rows, 0)
    x_spec[...] = dot(x_left[...], x_table[...])

    def spread(h, tile, first):
        for half in range(2):
            lanes = slice((h * 2 + half) * 128, (h * 2 + half + 1) * 128)
            pieces = [x_spec[pl.ds(pl.multiple_of((first + j) * 16, 16), 16), lanes] for j in range(8)]
            for i, piece in enumerate(block_swap(pieces)):
                f_send[tile, (half * 8 + i) * 16 : (half * 8 + i + 1) * 16, :] = piece

    def spread_chunk(h):
        lax.fori_loop(0, 4, lambda t, c: (spread(h, h * 5 + t, t * 8), c)[1], 0)

    spread_chunk(0)
    for half in range(2):
        pieces = [
            x_spec[(32 + j % 4) * 16 : (33 + j % 4) * 16, ((j // 4) * 2 + half) * 128 : ((j // 4) * 2 + half + 1) * 128]
            for j in range(8)
        ]
        for i, piece in enumerate(block_swap(pieces)):
            f_send[4, (half * 8 + i) * 16 : (half * 8 + i + 1) * 16, :] = piece

    pl.semaphore_wait(barrier, GZ - 1 + GY - 1)
    to_z[0][0]()
    spread_chunk(1)
    to_z[1][0]()

    def z_transform(table, source, result, tiles):
        lo, hi = tiles

        def fill(i, carry):
            lanes = pl.ds(pl.multiple_of(i * 128, 128), 128)
            for part in range(4):
                put_operand(z_right, part * 64, 256, lanes, source[lo + i, part * 64 : (part + 1) * 64, :])
            return carry

        lax.fori_loop(0, hi - lo, fill, 0)
        value = dot(table[...], z_right[:, 0 : (hi - lo) * 128])
        for i in range(hi - lo):
            result[lo + i] = value[:, i * 128 : (i + 1) * 128]

    def tile_of(h, t):
        return 4 if t == 4 else h * 5 + t

    def y_transform(h):
        for t in range(5):
            pieces = [g_recv[tile_of(h, t), pl.ds(k, GY, stride=8), :] for k in range(6)] + [None, None]
            swapped = block_swap(pieces)
            for b in range(8) if t < 4 else range(4):
                g = t * 8 + b
                c, y = g // YL, g % YL
                piece = swapped[b] if t < 4 else swapped[h * 4 + b]
                put_operand(y_right, y * GY, NY, slice(c * 128, (c + 1) * 128), piece)
        y_spec[...] = dot(y_fwd[...], y_right[...])

    def green(h):
        rows = 16
        lane = lane_ids(1)
        k8, part, z8 = lane % 8, (lane // 8) % 2, lane // 16
        wave_x = gz * 16 + h * 8 + k8
        wave_z = gy * 6 + z8
        signed_z = jnp.where(wave_z > NZ // 2, wave_z - NZ, wave_z)
        fx = jnp.broadcast_to(wave_x.astype(F32) / NX, (rows, 128))
        fz = jnp.broadcast_to(signed_z.astype(F32) / NZ, (rows, 128))
        lane_ok = (z8 < 6) & (wave_z != NZ // 2)
        weight = jnp.where(lane_ok, jnp.where(wave_x == 0, -1.0 / VOXELS, -2.0 / VOXELS), 0.0)
        origin = (wave_x == 0) & (wave_z == 0) & (z8 < 6)
        coupling = (lame_ref + shear_ref) / (shear_ref * (lame_ref + 2.0 * shear_ref))
        half_shear = 1.0 / (2.0 * shear_ref)

        def body(step, carry):
            start = pl.multiple_of(step * rows, rows)
            wave_y = start + lax.broadcasted_iota(jnp.int32, (rows, 128), 0)
            fy = jnp.where(wave_y > NY // 2, wave_y - NY, wave_y).astype(F32) / NY
            zero = origin & (wave_y == 0)
            keep = (wave_y != NY // 2) & jnp.logical_not(zero)
            norm = jnp.where(zero, 1.0, fx * fx + fy * fy + fz * fz)
            inverse = 1.0 / norm
            scale = jnp.where(keep, weight * inverse, 0.0)
            s = [y_spec[pl.ds(start, rows), c * 128 : (c + 1) * 128] for c in range(6)]
            vector = [
                fx * s[0] + fy * s[5] + fz * s[4],
                fx * s[5] + fy * s[1] + fz * s[3],
                fx * s[4] + fy * s[3] + fz * s[2],
            ]
            projected = fx * vector[0] + fy * vector[1] + fz * vector[2]
            fourth = (0.5 * coupling) * projected * inverse
            frequency = (fx, fy, fz)
            move = [scale * (half_shear * vector[i] - frequency[i] * fourth) for i in range(3)]
            images = [2.0 * frequency[i] * move[i] for i in range(3)]
            images += [frequency[i] * move[j] + frequency[j] * move[i] for i, j in ((1, 2), (0, 2), (0, 1))]
            real = (part == 0).astype(F32)
            gap = [target[c] * real - s[c] * (1.0 / VOXELS) for c in range(6)]
            gap_trace = (gap[0] + gap[1] + gap[2]) * (lame_ref / (3.0 * lame_ref + 2.0 * shear_ref))
            for c in range(6):
                macro = (gap[c] - gap_trace if c < 3 else gap[c]) * half_shear
                put_operand(y_right, start, NY, slice(c * 128, (c + 1) * 128), jnp.where(zero, macro, images[c]))
            return carry

        lax.fori_loop(0, NY // rows, body, 0)

    def y_inverse(h):
        y_lines[h] = dot(y_back[...], y_right[...])
        for t in range(4) if h == 0 else range(5):
            pieces = []
            for b in range(8):
                g = t * 8 + b if t < 4 else 32 + b % 4
                c, y = g // YL, g % YL
                source = h if t < 4 else b // 4
                pieces.append(y_lines[source, y * GY : (y + 1) * GY, c * 128 : (c + 1) * 128])
            swapped = block_swap(pieces)
            for k in range(6):
                h_send[tile_of(h, t), pl.ds(k, GY, stride=8), :] = swapped[k]

    def gather_half(tile, g, half, b_range, h):
        pieces = [b_recv[tile, (half * 8 + i) * 16 : (half * 8 + i + 1) * 16, :] for i in range(8)]
        swapped = block_swap(pieces)
        for n, b in enumerate(b_range):
            high, low = halves(swapped[b])
            rows = pl.ds(pl.multiple_of((g + n) * 16, 16), 16)
            for block, value in enumerate((high, low, high)):
                back_left[h, rows, block * 256 + half * 128 : block * 256 + (half + 1) * 128] = value

    def gather(h):
        def body(t, carry):
            for half in range(2):
                gather_half(h * 5 + t, t * 8, half, range(8), h)
            return carry

        lax.fori_loop(0, 4, body, 0)

    for load in loads:
        load.wait()

    to_z[0][1]()
    z_transform(z_fwd, f_recv, g_send, FORWARD[0])
    to_y[0][0]()
    to_y[0][1]()
    y_transform(0)
    green(0)
    y_inverse(0)
    from_y[0][0]()

    to_z[1][1]()
    z_transform(z_fwd, f_recv, g_send, FORWARD[1])
    to_y[1][0]()

    from_y[0][1]()
    z_transform(z_back, h_recv, b_send, BACKWARD[0])
    from_z[0][0]()

    to_y[1][1]()
    y_transform(1)
    green(1)
    y_inverse(1)
    from_y[1][0]()

    from_y[1][1]()
    z_transform(z_back, h_recv, b_send, BACKWARD[1])
    from_z[1][0]()

    from_z[0][1]()
    gather(0)
    x_spec[0:512, :] = dot(back_left[0, 0:512, :], x_back[0])
    from_z[1][1]()
    gather(1)
    for half in range(2):
        for h in range(2):
            gather_half(4, 32, half, range(h * 4, h * 4 + 4), h)
    x_spec[512:576, :] = dot(back_left[0, 512:576, :], x_back[0])
    x_spec[...] += dot(back_left[1], x_back[1])
    for c in range(6):
        for y in range(YL):
            g = c * YL + y
            out[c, y] = x_spec[g * 16 : g * 16 + ZL, :]

    for group in (to_z, to_y, from_y, from_z):
        for h in range(2):
            group[h][2]()


def local(strain, phase, density, target):
    consts = [jnp.asarray(table) for table in tables()]
    vmem = pl.BlockSpec(memory_space=pltpu.VMEM)
    smem = pl.BlockSpec(memory_space=pltpu.SMEM)
    hbm = pl.BlockSpec(memory_space=pl.ANY)
    dma = pltpu.SemaphoreType.DMA
    return pl.pallas_call(
        kernel,
        out_shape=jax.ShapeDtypeStruct((6, YL, ZL, NX), F32),
        in_specs=[vmem, vmem, smem, smem, vmem] + [hbm] * 5,
        out_specs=vmem,
        scratch_shapes=[pltpu.VMEM(table.shape, BF16) for table in consts[1:]]
        + [
            pltpu.VMEM((36, 16, NX), F32),
            pltpu.VMEM((576, 3 * NX), BF16),
            pltpu.VMEM((576, NX), F32),
        ]
        + [pltpu.VMEM((TILES, 256, 128), F32)] * 8
        + [
            pltpu.VMEM((1536, 640), BF16),
            pltpu.VMEM((6 * NY, 768), BF16),
            pltpu.VMEM((NY, 768), F32),
            pltpu.VMEM((2, NY, 768), F32),
            pltpu.VMEM((2, 576, 768), BF16),
        ]
        + [dma((5,))]
        + [dma((2, GZ)), dma((2, GZ)), dma((2, GY)), dma((2, GY)), dma((2, GY)), dma((2, GY)), dma((2, GZ)), dma((2, GZ))],
        compiler_params=pltpu.CompilerParams(collective_id=0, has_side_effects=True, vmem_limit_bytes=56 * 2**20),
        cost_estimate=pl.CostEstimate(flops=3_500_000_000, bytes_accessed=8_000_000, transcendentals=0),
    )(strain, phase, density, target, *consts)


def solution(mesh):
    placed = (P(None, "gy", "gz", None), P("gy", "gz", None), P(), P())
    return jax.shard_map(local, mesh=mesh, in_specs=placed, out_specs=P(None, "gy", "gz", None), check_vma=False)
```

time: 586 us -> 120 us (0.20); the launches traced: 576 us -> 119 us
  local copies, waits for them, and re-layouts: 189 us -> 2.42 us
  waiting for transfers between devices: 170 us -> 0 us
  Pallas kernels: 0 us -> 116 us
  blocking collectives: 115 us -> 0 us
  starting transfers between devices: 47.3 us -> 0 us
  other arithmetic: 25.7 us -> 0 us
  matrix products: 25.5 us -> 0 us
    all_to_all x4 -> x0, waiting for transfers between devices: 170 us -> none  [the longest x1 75.6 us: local(): lax.all_to_all(z_back, 'gz', split_axis=1, concat_axis=1, tiled=True)]
    pallas_call x0 -> x1, Pallas kernels: none -> 116 us  [local(): pl.pallas_call(kernel, out_shape=jax.ShapeDtypeStruct((6, YL, ZL, NX), F3...]
    psum x1 -> x0, blocking collectives: 115 us -> none  [local(): lax.psum((jnp.sum(strain, axis=(1, 2, 3)), jnp.sum(stress, axis=(1, 2, 3)...]
    reshape x8 -> x0, local copies, waits for them, and re-layouts: 92.4 us -> none  [the longest x2 34.3 us: local(): jnp.transpose(z_lines, (0, 4, 2, 3, 1, 5))]
    transpose x3 -> x0, local copies, waits for them, and re-layouts: 60.1 us -> none  [the longest x1 23.5 us: local(): jnp.transpose(back_z, (0, 5, 3, 2, 1, 4))]
    all_to_all x4 -> x0, starting transfers between devices: 47.3 us -> none  [the longest x1 13.3 us: local(): lax.all_to_all(y_spectrum, 'gz', split_axis=1, concat_axis=1, tiled=True)]
    dot_general x6 -> x0, matrix products: 25.5 us -> none  [contract(): jnp.einsum(form, left, right, precision=HIGHEST, preferred_element_type=j...]
    dot_general x5 -> x0, local copies, waits for them, and re-layouts: 19.9 us -> none  [contract(): jnp.einsum(form, left, right, precision=HIGHEST, preferred_element_type=j...]
  transfers between devices with their start and end apart: 4 -> 0, of which waited for: 3 -> 0; matrix products, arithmetic and copies ran while one was open for 3% -> 0% of each run, Pallas kernels for 0% -> 0%
where the time goes in v1:
time: 120 us; the launch traced here: 119 us
  Pallas kernels  116 us (97%)
  local copies, waits for them, and re-layouts  2.42 us (2%)
    pallas_call x1, Pallas kernels, local(): pl.pallas_call(kernel, out_shape=jax.ShapeDtypeStruct((6, YL, ZL, NX), F3...  116 us
    unnamed x1, local copies, waits for them, and re-layouts  2.42 us

profile of v1, /device:TPU:1, one launch (start us, length us, event | category | flops | bytes accessed | tf_op | source)
XLA Modules:
  0.0 118.6 jit_solution(18327178475913291053)
XLA Ops:
  0.0 116.2 %shard_map.100 = f32[6,6,12,512]{3,2,1,0:T(8,128)} custom-call(f32[6,6,12,512]{3,2,1,0:T(8,128)} %strain.1, s32[6,12,512]{2,1,0:T(8,128)} %phase.1, f32[16]{0:T(128)} %density.1, f32[6]{0:T(128)} %target.1, bf16[1536,512]{1,0:T(8,128)(2,1)} %constant.12.clone.x_table, bf16[256,1536]{1,0:T(8,128)(2,1)} %constant.13.clone.z_fwd_hbm, ...), custom_call_target="tpu_custom_call" | custom-call | flops 3500000000 | bytes 8000000 | tf_op jit(solution)/shard_map/pallas_call | solution.py:391
  116.2 2.4 %copy.12 = f32[6,6,12,512]{3,2,1,0:T(8,128)} copy(f32[6,6,12,512]{3,2,1,0:T(8,128)} %shard_map.100) | data formatting | bytes 1769472

commit v2 on v1

v2 whole, which is shorter than its diff:
```python
import math

import jax
import jax.numpy as jnp
import ml_dtypes
import numpy as np
from jax import lax
from jax.experimental import pallas as pl
from jax.experimental.pallas import tpu as pltpu
from jax.sharding import PartitionSpec as P

NX, NY, NZ = 512, 192, 192
GY, GZ = 32, 16
YL, ZL = NY // GY, NZ // GZ
VOXELS = float(NX * NY * NZ)
LAME_SOLID = 0.5769230769
SHEAR_SOLID = 0.3846153846
MESH = pl.DeviceIdType.MESH
F32, BF16 = jnp.float32, jnp.bfloat16
TILES = 9
CHUNKS = 4
FORWARD = ((0, 3), (3, 5), (5, 7), (7, 9))
BACKWARD = ((0, 2), (2, 4), (4, 6), (6, 9))
SHARED_FORWARD, SHARED_BACK = 2, 8


def forward_tile(h, t):
    return t if h == 0 else 1 + 2 * h + t


def group_row(c2, m):
    return c2 * 2 + m - 16 if m >= 16 else 4 + c2 * 16 + m


def split_table(table, axis):
    high = table.astype(np.float32).astype(ml_dtypes.bfloat16)
    low = (table - high.astype(np.float64)).astype(np.float32).astype(ml_dtypes.bfloat16)
    return np.concatenate([high, high, low], axis=axis)


def wave(rows, columns, length):
    angle = 2.0 * math.pi / length * ((np.asarray(rows)[:, None] * np.asarray(columns)[None, :]) % length)
    return np.cos(angle), np.sin(angle)


def tables():
    kx = np.array([d * 16 + h * 4 + k for h in range(CHUNKS) for d in range(GZ) for _ in range(2) for k in range(4)])
    imag = np.array([r for _ in range(CHUNKS) for _ in range(GZ) for r in range(2) for _ in range(4)])
    cosine, sine = wave(np.arange(NX), kx, NX)
    x_table = np.where(imag[None, :] == 0, cosine, -sine)
    x_forward = split_table(x_table, 0)
    x_back = np.stack([split_table(x_table.T[h * 128 : (h + 1) * 128], 0) for h in range(CHUNKS)])

    z_rows = np.arange(GZ * 16)
    z_of, z_ok = (z_rows // 16) * ZL + np.minimum(z_rows % 16, ZL - 1), z_rows % 16 < ZL
    k_rows = np.arange(GY * 8)
    k_of, k_ok = (k_rows // 8) * 6 + np.minimum(k_rows % 8, 5), k_rows % 8 < 6
    cosine, sine = wave(k_of, z_of, NZ)
    ok = k_ok[:, None] & z_ok[None, :]
    cosine, sine = np.where(ok, cosine, 0.0), np.where(ok, sine, 0.0)
    z_forward = split_table(np.concatenate([cosine, sine], axis=1), 1)
    z_back = split_table(np.concatenate([cosine.T, -sine.T], axis=1), 1)

    y_of = np.array([s * YL + y for y in range(YL) for s in range(GY)])
    cosine, sine = wave(np.arange(NY), y_of, NY)
    y_forward = split_table(np.concatenate([cosine, sine], axis=1), 1)
    y_back = split_table(np.concatenate([cosine.T, -sine.T], axis=1), 1)
    return x_forward, z_forward, y_forward, y_back, z_back, x_back


def lane_ids(rows):
    return lax.broadcasted_iota(jnp.int32, (rows, 128), 1)


def block_swap(arrays, width=8):
    lane = lane_ids(arrays[0].shape[0])
    step = len(arrays) // 2
    while step:
        shift = width * step
        low = (lane // shift) % 2 == 0
        out = list(arrays)
        for i in range(len(arrays)):
            if (i // step) % 2 == 0:
                a, b = arrays[i], arrays[i + step]
                out[i] = jnp.where(low, a, pltpu.roll(b, shift, 1))
                out[i + step] = jnp.where(low, pltpu.roll(a, 128 - shift, 1), b)
        arrays, step = out, step // 2
    return arrays


def pair_swap(a, b):
    low = lane_ids(a.shape[0]) < 64
    return jnp.where(low, a, pltpu.roll(b, 64, 1)), jnp.where(low, pltpu.roll(a, 64, 1), b)


def turned(x):
    real = (lane_ids(x.shape[0]) // 4) % 2 == 0
    return jnp.where(real, pltpu.roll(x, 124, 1), -pltpu.roll(x, 4, 1))


def halves(x):
    high = x.astype(BF16)
    return high, (x - high.astype(F32)).astype(BF16)


def put_operand(ref, row, count, lanes, x):
    high, low = halves(x)
    turn_high, turn_low = halves(turned(x))
    size = x.shape[0]
    for block, value in enumerate((high, turn_high, low, turn_low)):
        ref[pl.ds(row + block * count, size), lanes] = value


def dot(a, b):
    return jnp.dot(a, b, preferred_element_type=F32)


def dot_right(table, ref, lanes):
    cut = ref.shape[0]
    return dot(table[:, 0:cut], ref[:, lanes]) + dot(table[:, cut:], ref[0 : cut // 2, lanes])


def dot_left(left, table, lanes):
    cut = left.shape[1]
    return dot(left, table[0:cut, lanes]) + dot(left[:, 0 : cut // 2], table[cut:, lanes])


def kernel(
    strain, phase, density, target, x_table_hbm, z_fwd_hbm, y_fwd_hbm, y_back_hbm, z_back_hbm, x_back_hbm,
    out,
    x_table, z_fwd, y_fwd, y_back, z_back, x_back,
    field, x_left, x_spec,
    f_send, f_recv, g_send, g_recv, h_send, h_recv, b_send, b_recv,
    z_right, y_right, y_spec, y_lines, back_left,
    table_sem, f_ssem, f_rsem, g_ssem, g_rsem, h_ssem, h_rsem, b_ssem, b_rsem,
):
    gy, gz = lax.axis_index("gy"), lax.axis_index("gz")

    loads = [
        pltpu.make_async_copy(src, dst, table_sem.at[i])
        for i, (src, dst) in enumerate(
            ((x_table_hbm, x_table), (z_fwd_hbm, z_fwd), (y_fwd_hbm, y_fwd), (y_back_hbm, y_back), (z_back_hbm, z_back), (x_back_hbm, x_back))
        )
    ]
    for load in loads:
        load.start()

    f_recv[...] = jnp.zeros_like(f_recv)
    h_recv[...] = jnp.zeros_like(h_recv)

    barrier = pltpu.get_barrier_semaphore()

    def greet(axis, me, n):
        def body(i, carry):
            pl.semaphore_signal(barrier, inc=1, device_id={axis: lax.rem(me + i, n)}, device_id_type=MESH)
            return carry

        lax.fori_loop(1, n, body, 0)

    greet("gz", gz, GZ)
    greet("gy", gy, GY)

    def transfer(axis, me, n, pad, used, src, dst, ssem, rsem, chunk, tiles):
        lo, hi = tiles

        def copy(i):
            hop = lax.div(i + 1, 2)
            there = lax.rem(me + jnp.where(lax.rem(i, 2) == 1, hop, n - hop), n)
            return pltpu.make_async_remote_copy(
                src_ref=src.at[lo:hi, pl.ds(pl.multiple_of(there * pad, pad), used), :],
                dst_ref=dst.at[lo:hi, pl.ds(pl.multiple_of(me * pad, pad), used), :],
                send_sem=ssem.at[chunk, i],
                recv_sem=rsem.at[chunk, i],
                device_id={axis: there},
                device_id_type=MESH,
            )

        def start():
            lax.fori_loop(1, n, lambda i, c: (copy(i).start(), c)[1], 0)
            own = pl.ds(pl.multiple_of(me * pad, pad), used)
            dst[lo:hi, own, :] = src[lo:hi, own, :]

        def wait_recv():
            lax.fori_loop(1, n, lambda i, c: (copy(i).wait_recv(), c)[1], 0)

        def wait_send():
            lax.fori_loop(1, n, lambda i, c: (copy(i).wait_send(), c)[1], 0)

        return start, wait_recv, wait_send

    to_z = [transfer("gz", gz, GZ, 16, ZL, f_send, f_recv, f_ssem, f_rsem, h, FORWARD[h]) for h in range(CHUNKS)]
    to_y = [transfer("gy", gy, GY, 8, 6, g_send, g_recv, g_ssem, g_rsem, h, FORWARD[h]) for h in range(CHUNKS)]
    from_y = [transfer("gy", gy, GY, 8, 6, h_send, h_recv, h_ssem, h_rsem, h, BACKWARD[h]) for h in range(CHUNKS)]
    from_z = [transfer("gz", gz, GZ, 16, ZL, b_send, b_recv, b_ssem, b_rsem, h, BACKWARD[h]) for h in range(CHUNKS)]

    cubes = [density[i] * density[i] * density[i] for i in range(16)]
    least, most = cubes[0], cubes[0]
    for value in cubes[1:]:
        least, most = jnp.minimum(least, value), jnp.maximum(most, value)
    middle = 0.5 * (least + most)
    lame_ref, shear_ref = LAME_SOLID * middle, SHEAR_SOLID * middle

    field[...] = jnp.zeros_like(field)

    def polarize(y, carry):
        level = phase[y]
        stiff = jnp.zeros(level.shape, F32)
        for i, value in enumerate(cubes):
            stiff = jnp.where(level == i, value, stiff)
        excess = stiff - middle
        parts = [strain[c, y] for c in range(6)]
        trace = LAME_SOLID * (parts[0] + parts[1] + parts[2])
        for c in range(6):
            value = (2.0 * SHEAR_SOLID) * parts[c]
            m = (c // 2) * YL + y
            row = jnp.where(m >= 16, c % 2 * 2 + m - 16, 4 + c % 2 * 16 + m)
            field[row, 0:ZL, :] = excess * (value + trace if c < 3 else value)
        return carry

    lax.fori_loop(0, YL, polarize, 0)

    def split_rows(g, carry):
        high, low = halves(field[g])
        rows = pl.ds(pl.multiple_of(g * 16, 16), 16)
        x_left[rows, 0:512] = high
        x_left[rows, 512:1024] = low
        return carry

    lax.fori_loop(0, 36, split_rows, 0)

    def x_transform(rows, lanes):
        x_spec[rows, lanes] = dot_left(x_left[rows, :], x_table, lanes)

    def x_piece(c2, m, h):
        row = group_row(c2, m) * 16
        return x_spec[row : row + 16, h * 128 : (h + 1) * 128]

    def send_tile(tile, pieces):
        for i, piece in enumerate(block_swap(pieces)):
            f_send[tile, i * 16 : (i + 1) * 16, :] = piece

    def spread(h):
        for t in range(2):
            send_tile(forward_tile(h, t), [x_piece(c2, t * 8 + b, h) for c2 in range(2) for b in range(8)])

    loads[0].wait()
    x_transform(slice(0, 576), slice(0, 128))
    x_transform(slice(0, 64), slice(128, 512))
    spread(0)
    send_tile(SHARED_FORWARD, [x_piece(c2, 16 + e, h) for c2 in range(2) for h in range(CHUNKS) for e in range(2)])
    pl.semaphore_wait(barrier, GZ - 1 + GY - 1)
    to_z[0][0]()
    for h in range(1, CHUNKS):
        x_transform(slice(64, 576), slice(h * 128, (h + 1) * 128))
        spread(h)
        to_z[h][0]()

    def z_transform(table, source, result, tiles):
        lo, hi = tiles

        def fill(i, carry):
            lanes = pl.ds(pl.multiple_of(i * 128, 128), 128)
            for part in range(4):
                put_operand(z_right, part * 64, 256, lanes, source[lo + i, part * 64 : (part + 1) * 64, :])
            return carry

        lax.fori_loop(0, hi - lo, fill, 0)
        value = dot_right(table, z_right, slice(0, (hi - lo) * 128))
        for i in range(hi - lo):
            result[lo + i] = value[:, i * 128 : (i + 1) * 128]

    def y_transform(h):
        def unpack(tile):
            pieces = [g_recv[tile, pl.ds(k, GY, stride=8), :] for k in range(6)]
            return block_swap(pieces + [jnp.zeros((GY, 128), F32)] * 2)

        for t in range(3):
            swapped = unpack(forward_tile(h, t)) if t < 2 else unpack(SHARED_FORWARD)[h * 2 : h * 2 + 2]
            for b, piece in enumerate(swapped):
                cp, y = (t * 8 + b) // YL, (t * 8 + b) % YL
                put_operand(y_right, y * GY, NY, slice(cp * 128, (cp + 1) * 128), piece)
        y_spec[...] = dot_right(y_fwd, y_right, slice(0, 384))

    def green(h):
        rows = 16
        lane = lane_ids(1)
        k4, part, z8 = lane % 4, (lane // 4) % 2, (lane // 8) % 8
        wave_x = gz * 16 + h * 4 + k4
        wave_z = gy * 6 + z8
        signed_z = jnp.where(wave_z > NZ // 2, wave_z - NZ, wave_z)
        fx = jnp.broadcast_to(wave_x.astype(F32) / NX, (rows, 128))
        fz = jnp.broadcast_to(signed_z.astype(F32) / NZ, (rows, 128))
        lane_ok = (z8 < 6) & (wave_z != NZ // 2)
        weight = jnp.where(lane_ok, jnp.where(wave_x == 0, -1.0 / VOXELS, -2.0 / VOXELS), 0.0)
        origin = (wave_x == 0) & (wave_z == 0) & (z8 < 6)
        coupling = (lame_ref + shear_ref) / (shear_ref * (lame_ref + 2.0 * shear_ref))
        half_shear = 1.0 / (2.0 * shear_ref)

        def body(step, carry):
            start = pl.multiple_of(step * rows, rows)
            upper = pl.multiple_of(start + NY // 2, rows)
            wave_y = start + lax.broadcasted_iota(jnp.int32, (rows, 128), 0)
            wave_y = wave_y + jnp.where(lane_ids(rows) < 64, 0, NY // 2)
            fy = jnp.where(wave_y > NY // 2, wave_y - NY, wave_y).astype(F32) / NY
            zero = origin & (wave_y == 0)
            keep = (wave_y != NY // 2) & jnp.logical_not(zero)
            norm = jnp.where(zero, 1.0, fx * fx + fy * fy + fz * fz)
            inverse = 1.0 / norm
            scale = jnp.where(keep, weight * inverse, 0.0)
            s = []
            for cp in range(3):
                lanes = slice(cp * 128, (cp + 1) * 128)
                s += pair_swap(y_spec[pl.ds(start, rows), lanes], y_spec[pl.ds(upper, rows), lanes])
            vector = [
                fx * s[0] + fy * s[5] + fz * s[4],
                fx * s[5] + fy * s[1] + fz * s[3],
                fx * s[4] + fy * s[3] + fz * s[2],
            ]
            projected = fx * vector[0] + fy * vector[1] + fz * vector[2]
            fourth = (0.5 * coupling) * projected * inverse
            frequency = (fx, fy, fz)
            move = [scale * (half_shear * vector[i] - frequency[i] * fourth) for i in range(3)]
            images = [2.0 * frequency[i] * move[i] for i in range(3)]
            images += [frequency[i] * move[j] + frequency[j] * move[i] for i, j in ((1, 2), (0, 2), (0, 1))]
            real = (part == 0).astype(F32)
            gap = [target[c] * real - s[c] * (1.0 / VOXELS) for c in range(6)]
            gap_trace = (gap[0] + gap[1] + gap[2]) * (lame_ref / (3.0 * lame_ref + 2.0 * shear_ref))
            for c in range(6):
                macro = (gap[c] - gap_trace if c < 3 else gap[c]) * half_shear
                images[c] = jnp.where(zero, macro, images[c])
            for cp in range(3):
                lanes = slice(cp * 128, (cp + 1) * 128)
                first, second = pair_swap(images[2 * cp], images[2 * cp + 1])
                put_operand(y_right, start, NY, lanes, first)
                put_operand(y_right, upper, NY, lanes, second)
            return carry

        lax.fori_loop(0, NY // 2 // rows, body, 0)

    def y_inverse(h):
        y_lines[h] = dot_right(y_back, y_right, slice(0, 384))

        def line(chunk, m):
            cp, y = m // YL, m % YL
            return y_lines[chunk, y * GY : (y + 1) * GY, cp * 128 : (cp + 1) * 128]

        def pack(tile, pieces):
            swapped = block_swap(pieces)
            for k in range(6):
                h_send[tile, pl.ds(k, GY, stride=8), :] = swapped[k]

        for t in range(2):
            pack(2 * h + t, [line(h, t * 8 + b) for b in range(8)])
        if h == CHUNKS - 1:
            pack(SHARED_BACK, [line(chunk, 16 + e) for chunk in range(CHUNKS) for e in range(2)])

    def gather(tile, places):
        swapped = block_swap([b_recv[tile, i * 16 : (i + 1) * 16, :] for i in range(GZ)])
        for (h, row), piece in zip(places, swapped, strict=True):
            high, low = halves(piece)
            back_left[h, row * 16 : (row + 1) * 16, 0:128] = high
            back_left[h, row * 16 : (row + 1) * 16, 128:256] = low

    def x_inverse(h):
        for t in range(2):
            gather(2 * h + t, [(h, group_row(c2, t * 8 + b)) for c2 in range(2) for b in range(8)])
        value = dot_left(back_left[h, 64:576, :], x_back.at[h], slice(0, NX))
        x_spec[64:576, :] = value if h == 0 else x_spec[64:576, :] + value

    def x_shared():
        gather(
            SHARED_BACK,
            [(h, group_row(c2, 16 + e)) for c2 in range(2) for h in range(CHUNKS) for e in range(2)],
        )
        x_spec[0:64, :] = sum(dot_left(back_left[h, 0:64, :], x_back.at[h], slice(0, NX)) for h in range(CHUNKS))

    for load in loads[1:]:
        load.wait()

    def stage_z(h):
        to_z[h][1]()
        z_transform(z_fwd, f_recv, g_send, FORWARD[h])
        to_y[h][0]()

    def stage_y(h):
        to_y[h][1]()
        y_transform(h)
        green(h)
        y_inverse(h)
        from_y[h][0]()

    def stage_back(h):
        from_y[h][1]()
        z_transform(z_back, h_recv, b_send, BACKWARD[h])
        from_z[h][0]()

    def stage_x(h):
        from_z[h][1]()
        x_inverse(h)

    stage_z(0)
    stage_z(1)
    stage_y(0)
    stage_z(2)
    stage_y(1)
    stage_back(0)
    stage_z(3)
    stage_y(2)
    stage_back(1)
    stage_y(3)
    stage_back(2)
    stage_x(0)
    stage_back(3)
    stage_x(1)
    stage_x(2)
    for group in (to_z, to_y, from_y, from_z):
        for h in range(CHUNKS - (group is from_z)):
            group[h][2]()
    stage_x(3)
    x_shared()
    for c in range(6):
        for y in range(YL):
            row = group_row(c % 2, c // 2 * YL + y) * 16
            out[c, y] = x_spec[row : row + ZL, :]
    from_z[CHUNKS - 1][2]()


def local(strain, phase, density, target):
    consts = [jnp.asarray(table) for table in tables()]
    vmem = pl.BlockSpec(memory_space=pltpu.VMEM)
    smem = pl.BlockSpec(memory_space=pltpu.SMEM)
    hbm = pl.BlockSpec(memory_space=pl.ANY)
    dma = pltpu.SemaphoreType.DMA
    return pl.pallas_call(
        kernel,
        out_shape=jax.ShapeDtypeStruct((6, YL, ZL, NX), F32),
        in_specs=[vmem, vmem, smem, smem] + [hbm] * 6,
        out_specs=vmem,
        scratch_shapes=[pltpu.VMEM(table.shape, BF16) for table in consts]
        + [
            pltpu.VMEM((36, 16, NX), F32),
            pltpu.VMEM((576, 2 * NX), BF16),
            pltpu.VMEM((576, NX), F32),
        ]
        + [pltpu.VMEM((TILES, 256, 128), F32)] * 8
        + [
            pltpu.VMEM((1024, 384), BF16),
            pltpu.VMEM((4 * NY, 384), BF16),
            pltpu.VMEM((NY, 384), F32),
            pltpu.VMEM((CHUNKS, NY, 384), F32),
            pltpu.VMEM((CHUNKS, 576, 256), BF16),
        ]
        + [dma((6,))]
        + [dma((CHUNKS, n)) for n in (GZ, GZ, GY, GY, GY, GY, GZ, GZ)],
        compiler_params=pltpu.CompilerParams(collective_id=0, has_side_effects=True, vmem_limit_bytes=56 * 2**20),
        cost_estimate=pl.CostEstimate(flops=3_500_000_000, bytes_accessed=8_000_000, transcendentals=0),
    )(strain, phase, density, target, *consts)


def solution(mesh):
    placed = (P(None, "gy", "gz", None), P("gy", "gz", None), P(), P())
    return jax.shard_map(local, mesh=mesh, in_specs=placed, out_specs=P(None, "gy", "gz", None), check_vma=False)
```

time: 120 us -> 113 us (0.942); the launches traced: 119 us -> 113 us
  Pallas kernels: 116 us -> 111 us
    pallas_call x1, Pallas kernels: 116 us -> 111 us  [local(): pl.pallas_call(kernel, out_shape=jax.ShapeDtypeStruct((6, YL, ZL, NX), F3...]
where the time goes in v2:
time: 113 us
  Pallas kernels  111 us (98%)
  local copies, waits for them, and re-layouts  2.42 us (2%)
    pallas_call x1, Pallas kernels, local(): pl.pallas_call(kernel, out_shape=jax.ShapeDtypeStruct((6, YL, ZL, NX), F3...  111 us
    unnamed x1, local copies, waits for them, and re-layouts  2.42 us

profile of v2, /device:TPU:1, one launch (start us, length us, event | category | flops | bytes accessed | tf_op | source)
XLA Modules:
  0.0 113.2 jit_solution(9535848230405447268)
XLA Ops:
  0.0 110.7 %shard_map.100 = f32[6,6,12,512]{3,2,1,0:T(8,128)} custom-call(f32[6,6,12,512]{3,2,1,0:T(8,128)} %strain.1, s32[6,12,512]{2,1,0:T(8,128)} %phase.1, f32[16]{0:T(128)} %density.1, f32[6]{0:T(128)} %target.1, bf16[1536,512]{1,0:T(8,128)(2,1)} %constant.12.clone.x_table_hbm, bf16[256,1536]{1,0:T(8,128)(2,1)} %constant.13.clone.z_fwd_hbm, ...), custom_call_target="tpu_custom_call" | custom-call | flops 3500000000 | bytes 8000000 | tf_op jit(solution)/shard_map/pallas_call | solution.py:434
  110.8 2.4 %copy.12 = f32[6,6,12,512]{3,2,1,0:T(8,128)} copy(f32[6,6,12,512]{3,2,1,0:T(8,128)} %shard_map.100) | data formatting | bytes 1769472

commit v3 on v2

--- a/solution.py
+++ b/solution.py
@@ -164,13 +164,13 @@
         lo, hi = tiles
 
         def copy(i):
-            hop = lax.div(i + 1, 2)
+            hop = n // 2 - lax.div(i, 2)
             there = lax.rem(me + jnp.where(lax.rem(i, 2) == 1, hop, n - hop), n)
             return pltpu.make_async_remote_copy(
                 src_ref=src.at[lo:hi, pl.ds(pl.multiple_of(there * pad, pad), used), :],
                 dst_ref=dst.at[lo:hi, pl.ds(pl.multiple_of(me * pad, pad), used), :],
-                send_sem=ssem.at[chunk, i],
-                recv_sem=rsem.at[chunk, i],
+                send_sem=ssem.at[chunk],
+                recv_sem=rsem.at[chunk],
                 device_id={axis: there},
                 device_id_type=MESH,
             )
@@ -180,11 +180,22 @@
             own = pl.ds(pl.multiple_of(me * pad, pad), used)
             dst[lo:hi, own, :] = src[lo:hi, own, :]
 
+        def all_copies():
+            rows = (n - 1) * used
+            return pltpu.make_async_remote_copy(
+                src_ref=src.at[lo:hi, 0:rows, :],
+                dst_ref=dst.at[lo:hi, 0:rows, :],
+                send_sem=ssem.at[chunk],
+                recv_sem=rsem.at[chunk],
+                device_id={axis: lax.rem(me + 1, n)},
+                device_id_type=MESH,
+            )
+
         def wait_recv():
-            lax.fori_loop(1, n, lambda i, c: (copy(i).wait_recv(), c)[1], 0)
+            all_copies().wait_recv()
 
         def wait_send():
-            lax.fori_loop(1, n, lambda i, c: (copy(i).wait_send(), c)[1], 0)
+            all_copies().wait_send()
 
         return start, wait_recv, wait_send
 
@@ -451,7 +462,7 @@
             pltpu.VMEM((CHUNKS, 576, 256), BF16),
         ]
         + [dma((6,))]
-        + [dma((CHUNKS, n)) for n in (GZ, GZ, GY, GY, GY, GY, GZ, GZ)],
+        + [dma((CHUNKS,))] * 8,
         compiler_params=pltpu.CompilerParams(collective_id=0, has_side_effects=True, vmem_limit_bytes=56 * 2**20),
         cost_estimate=pl.CostEstimate(flops=3_500_000_000, bytes_accessed=8_000_000, transcendentals=0),
     )(strain, phase, density, target, *consts)

time: 113 us -> 102 us (0.903)
  Pallas kernels: 111 us -> 99.8 us
    pallas_call x1, Pallas kernels: 111 us -> 99.8 us  [local(): pl.pallas_call(kernel, out_shape=jax.ShapeDtypeStruct((6, YL, ZL, NX), F3...]
where the time goes in v3:
time: 102 us
  Pallas kernels  99.8 us (98%)
  local copies, waits for them, and re-layouts  2.42 us (2%)
    pallas_call x1, Pallas kernels, local(): pl.pallas_call(kernel, out_shape=jax.ShapeDtypeStruct((6, YL, ZL, NX), F3...  99.8 us
    unnamed x1, local copies, waits for them, and re-layouts  2.42 us

profile of v3, /device:TPU:1, one launch (start us, length us, event | category | flops | bytes accessed | tf_op | source)
XLA Modules:
  0.0 102.2 jit_solution(9186074366785968203)
XLA Ops:
  0.0 99.8 %shard_map.100 = f32[6,6,12,512]{3,2,1,0:T(8,128)} custom-call(f32[6,6,12,512]{3,2,1,0:T(8,128)} %strain.1, s32[6,12,512]{2,1,0:T(8,128)} %phase.1, f32[16]{0:T(128)} %density.1, f32[6]{0:T(128)} %target.1, bf16[1536,512]{1,0:T(8,128)(2,1)} %constant.12.clone.x_table_hbm, bf16[256,1536]{1,0:T(8,128)(2,1)} %constant.13.clone.z_fwd_hbm, ...), custom_call_target="tpu_custom_call" | custom-call | flops 3500000000 | bytes 8000000 | tf_op jit(solution)/shard_map/pallas_call | solution.py:445
  99.8 2.4 %copy.12 = f32[6,6,12,512]{3,2,1,0:T(8,128)} copy(f32[6,6,12,512]{3,2,1,0:T(8,128)} %shard_map.100) | data formatting | bytes 1769472

commit v4 on v3

--- a/solution.py
+++ b/solution.py
@@ -126,9 +126,9 @@
 
 
 def kernel(
-    strain, phase, density, target, x_table_hbm, z_fwd_hbm, y_fwd_hbm, y_back_hbm, z_back_hbm, x_back_hbm,
+    strain_hbm, phase_hbm, density, target, x_table_hbm, z_fwd_hbm, y_fwd_hbm, y_back_hbm, z_back_hbm, x_back_hbm,
     out,
-    x_table, z_fwd, y_fwd, y_back, z_back, x_back,
+    strain, phase, x_table, z_fwd, y_fwd, y_back, z_back, x_back,
     field, x_left, x_spec,
     f_send, f_recv, g_send, g_recv, h_send, h_recv, b_send, b_recv,
     z_right, y_right, y_spec, y_lines, back_left,
@@ -139,15 +139,12 @@
     loads = [
         pltpu.make_async_copy(src, dst, table_sem.at[i])
         for i, (src, dst) in enumerate(
-            ((x_table_hbm, x_table), (z_fwd_hbm, z_fwd), (y_fwd_hbm, y_fwd), (y_back_hbm, y_back), (z_back_hbm, z_back), (x_back_hbm, x_back))
+            ((strain_hbm, strain), (phase_hbm, phase), (x_table_hbm, x_table), (z_fwd_hbm, z_fwd), (y_fwd_hbm, y_fwd), (y_back_hbm, y_back), (z_back_hbm, z_back), (x_back_hbm, x_back))
         )
     ]
     for load in loads:
         load.start()
 
-    f_recv[...] = jnp.zeros_like(f_recv)
-    h_recv[...] = jnp.zeros_like(h_recv)
-
     barrier = pltpu.get_barrier_semaphore()
 
     def greet(axis, me, n):
@@ -159,6 +156,11 @@
 
     greet("gz", gz, GZ)
     greet("gy", gy, GY)
+
+    for i in range(GZ):
+        f_recv[:, i * 16 + ZL : (i + 1) * 16, :] = jnp.zeros((TILES, 16 - ZL, 128), F32)
+    for i in range(GY):
+        h_recv[:, i * 8 + 6 : (i + 1) * 8, :] = jnp.zeros((TILES, 2, 128), F32)
 
     def transfer(axis, me, n, pad, used, src, dst, ssem, rsem, chunk, tiles):
         lo, hi = tiles
@@ -212,6 +214,8 @@
     lame_ref, shear_ref = LAME_SOLID * middle, SHEAR_SOLID * middle
 
     field[...] = jnp.zeros_like(field)
+    loads[0].wait()
+    loads[1].wait()
 
     def polarize(y, carry):
         level = phase[y]
@@ -254,7 +258,7 @@
         for t in range(2):
             send_tile(forward_tile(h, t), [x_piece(c2, t * 8 + b, h) for c2 in range(2) for b in range(8)])
 
-    loads[0].wait()
+    loads[2].wait()
     x_transform(slice(0, 576), slice(0, 128))
     x_transform(slice(0, 64), slice(128, 512))
     spread(0)
@@ -385,7 +389,7 @@
         )
         x_spec[0:64, :] = sum(dot_left(back_left[h, 0:64, :], x_back.at[h], slice(0, NX)) for h in range(CHUNKS))
 
-    for load in loads[1:]:
+    for load in loads[3:]:
         load.wait()
 
     def stage_z(h):
@@ -440,14 +444,15 @@
     consts = [jnp.asarray(table) for table in tables()]
     vmem = pl.BlockSpec(memory_space=pltpu.VMEM)
     smem = pl.BlockSpec(memory_space=pltpu.SMEM)
-    hbm = pl.BlockSpec(memory_space=pl.ANY)
+    hbm = pl.BlockSpec(memory_space=pltpu.HBM)
     dma = pltpu.SemaphoreType.DMA
     return pl.pallas_call(
         kernel,
-        out_shape=jax.ShapeDtypeStruct((6, YL, ZL, NX), F32),
-        in_specs=[vmem, vmem, smem, smem] + [hbm] * 6,
+        out_shape=pltpu.VMEM((6, YL, ZL, NX), F32),
+        in_specs=[hbm, hbm, smem, smem] + [hbm] * 6,
         out_specs=vmem,
-        scratch_shapes=[pltpu.VMEM(table.shape, BF16) for table in consts]
+        scratch_shapes=[pltpu.VMEM((6, YL, ZL, NX), F32), pltpu.VMEM((YL, ZL, NX), jnp.int32)]
+        + [pltpu.VMEM(table.shape, BF16) for table in consts]
         + [
             pltpu.VMEM((36, 16, NX), F32),
             pltpu.VMEM((576, 2 * NX), BF16),
@@ -461,7 +466,7 @@
             pltpu.VMEM((CHUNKS, NY, 384), F32),
             pltpu.VMEM((CHUNKS, 576, 256), BF16),
         ]
-        + [dma((6,))]
+        + [dma((8,))]
         + [dma((CHUNKS,))] * 8,
         compiler_params=pltpu.CompilerParams(collective_id=0, has_side_effects=True, vmem_limit_bytes=56 * 2**20),
         cost_estimate=pl.CostEstimate(flops=3_500_000_000, bytes_accessed=8_000_000, transcendentals=0),

time: 102 us -> 99.3 us (0.974)
  Pallas kernels: 99.8 us -> 98.1 us
  local copies, waits for them, and re-layouts: 2.42 us -> 1.02 us
    pallas_call x1, Pallas kernels: 99.8 us -> 98.1 us  [local(): pl.pallas_call(kernel, out_shape=pltpu.VMEM((6, YL, ZL, NX), F32), in_spe...]
    unnamed x1, local copies, waits for them, and re-layouts: 2.42 us -> 1.02 us
where the time goes in v4:
time: 99.3 us; the launch traced here: 99.1 us
  Pallas kernels  98.1 us (99%)
  local copies, waits for them, and re-layouts  1.02 us (1%)
    pallas_call x1, Pallas kernels, local(): pl.pallas_call(kernel, out_shape=pltpu.VMEM((6, YL, ZL, NX), F32), in_spe...  98.1 us

profile of v4, /device:TPU:1, one launch (start us, length us, event | category | flops | bytes accessed | tf_op | source)
XLA Modules:
  0.0 99.1 jit_solution(78138078846961304)
XLA Ops:
  0.0 98.1 %shard_map.100 = f32[6,6,12,512]{3,2,1,0:T(8,128)S(1)} custom-call(f32[6,6,12,512]{3,2,1,0:T(8,128)} %strain_hbm.1, s32[6,12,512]{2,1,0:T(8,128)} %phase_hbm.1, f32[16]{0:T(128)} %density.1, f32[6]{0:T(128)} %target.1, bf16[1536,512]{1,0:T(8,128)(2,1)} %constant.12.clone.x_table_hbm, bf16[256,1536]{1,0:T(8,128)(2,1)} %constant.13.clone.z_fwd_hbm, ...), custom_call_target="tpu_custom_call" | custom-call | flops 3500000000 | bytes 8000000 | tf_op jit(solution)/shard_map/pallas_call | solution.py:449
  98.1 1.0 %copy.12 = f32[6,6,12,512]{3,2,1,0:T(8,128)} copy(f32[6,6,12,512]{3,2,1,0:T(8,128)S(1)} %shard_map.100) | data formatting | bytes 1769472

commit v5 on v4

--- a/solution.py
+++ b/solution.py
@@ -165,9 +165,22 @@
     def transfer(axis, me, n, pad, used, src, dst, ssem, rsem, chunk, tiles):
         lo, hi = tiles
 
-        def copy(i):
+        def far_first(i):
             hop = n // 2 - lax.div(i, 2)
-            there = lax.rem(me + jnp.where(lax.rem(i, 2) == 1, hop, n - hop), n)
+            return lax.rem(me + jnp.where(lax.rem(i, 2) == 1, hop, n - hop), n)
+
+        def start_ordered(i, carry):
+            quarter = lax.div(i, 4)
+            quarter = lax.rem(quarter, 2) * 2 + lax.div(quarter, 2)
+            there = quarter * 4 + lax.rem(me + i, 4)
+
+            @pl.when(there != me)
+            def _():
+                copy_to(there).start()
+
+            return carry
+
+        def copy_to(there):
             return pltpu.make_async_remote_copy(
                 src_ref=src.at[lo:hi, pl.ds(pl.multiple_of(there * pad, pad), used), :],
                 dst_ref=dst.at[lo:hi, pl.ds(pl.multiple_of(me * pad, pad), used), :],
@@ -178,7 +191,10 @@
             )
 
         def start():
-            lax.fori_loop(1, n, lambda i, c: (copy(i).start(), c)[1], 0)
+            if src is b_send and chunk == CHUNKS - 1:
+                lax.fori_loop(0, n, start_ordered, 0)
+            else:
+                lax.fori_loop(1, n, lambda i, c: (copy_to(far_first(i)).start(), c)[1], 0)
             own = pl.ds(pl.multiple_of(me * pad, pad), used)
             dst[lo:hi, own, :] = src[lo:hi, own, :]
 

time: 99.3 us -> 95.9 us (0.966)
  Pallas kernels: 98.1 us -> 94 us
    pallas_call x1, Pallas kernels: 98.1 us -> 94 us  [local(): pl.pallas_call(kernel, out_shape=pltpu.VMEM((6, YL, ZL, NX), F32), in_spe...]
where the time goes in v5:
time: 95.9 us; the launch traced here: 95 us
  Pallas kernels  94 us (98%)
  local copies, waits for them, and re-layouts  1.02 us (1%)
    pallas_call x1, Pallas kernels, local(): pl.pallas_call(kernel, out_shape=pltpu.VMEM((6, YL, ZL, NX), F32), in_spe...  94 us

profile of v5, /device:TPU:1, one launch (start us, length us, event | category | flops | bytes accessed | tf_op | source)
XLA Modules:
  0.0 95.0 jit_solution(4941405539211004880)
XLA Ops:
  0.0 94.0 %shard_map.100 = f32[6,6,12,512]{3,2,1,0:T(8,128)S(1)} custom-call(f32[6,6,12,512]{3,2,1,0:T(8,128)} %strain_hbm.1, s32[6,12,512]{2,1,0:T(8,128)} %phase_hbm.1, f32[16]{0:T(128)} %density.1, f32[6]{0:T(128)} %target.1, bf16[1536,512]{1,0:T(8,128)(2,1)} %constant.12.clone.x_table_hbm, bf16[256,1536]{1,0:T(8,128)(2,1)} %constant.13.clone.z_fwd_hbm, ...), custom_call_target="tpu_custom_call" | custom-call | flops 3500000000 | bytes 8000000 | tf_op jit(solution)/shard_map/pallas_call | solution.py:465
  94.0 1.0 %copy.12 = f32[6,6,12,512]{3,2,1,0:T(8,128)} copy(f32[6,6,12,512]{3,2,1,0:T(8,128)S(1)} %shard_map.100) | data formatting | bytes 1769472
